TPU v7x, 32 devices: a whole 2x2x4 slice. The times are simulated.
32 devices in a mesh: ma: 8 (over z, x), pol: 4 (over y, core).
Axes of the slice: x: 2, y: 2, z: 4, core: 2. Of those that a mesh axis runs over, the one named last changes fastest.
Arguments:
- sky_coeffs: bfloat16 [64, 4096], P('ma'), may hold values from -6 to 6
- visibilities: bfloat16 [64, 512], P('ma', 'pol'), may hold values from -6 to 6
- beam_blocks: bfloat16 [64, 512, 4096], P('ma', 'pol'), may hold values from -0.09375 to 0.09375
- mode_counts: int32 [64], P('ma'), may hold values from 128 to 512, as said below
- order_table: int32 [64], replicated, may hold values from 0 to 2047, as said below
- band_limits: int32 [8, 2], replicated, may hold values from 0 to 2048, as said below
Outputs:
- gradient: float32 [64, 4096], P('ma', 'pol')
Inputs may be any that keep to these rules, and one draw needn't show every extreme that they name: `mode_counts`: the number of leading modes kept for the order of that row; some row keeps all 512. `order_table`: all entries differ. `band_limits`: row j is (low, high) with high - low between 512 and 1024.
All inputs are finite; a program needn't handle non-finite values.
Results may differ from a plain program's by a relative error of at most 0.0023.
Values may be sent and summed in bfloat16 or wider, within the bound.
A program may use at most 192 MiB of HBM per device.

v0:
```python
import functools
import math

import jax
import jax.numpy as jnp
from jax import lax
from jax.experimental import pallas as pl
from jax.experimental.pallas import tpu as pltpu
from jax.sharding import PartitionSpec as P

L = 2048
J = 8
CYCLES = 2 * L
FINE_ELL = 32
PIX_FINE = 128
PIX_TILE = 512
MESH = pl.DeviceIdType.MESH

smoothing = 0.1
prior_weight = 0.2


def order_phases(orders):
    quarter = jnp.mod(orders, 4)
    cos_phase = (quarter == 0).astype(jnp.float32) - (quarter == 2).astype(jnp.float32)
    sin_phase = (quarter == 1).astype(jnp.float32) - (quarter == 3).astype(jnp.float32)
    return (cos_phase, sin_phase)


def band_kernel(limits):
    ell_index = jnp.arange(L, dtype=jnp.int32)[None, :]
    low_edge = limits[:, 0:1]
    high_edge = limits[:, 1:2]
    fraction = (ell_index - low_edge).astype(jnp.float32) / (high_edge - low_edge).astype(
        jnp.float32
    )
    inside = (ell_index >= low_edge) & (ell_index <= high_edge)
    return jnp.where(inside, jnp.sin(jnp.pi * fraction) ** 2, 0.0)


def cycle_weights(cycle_start, cycle_count):
    cycle_index = cycle_start + jnp.arange(cycle_count, dtype=jnp.int32)
    return jnp.sin(jnp.pi * (2 * cycle_index + 1).astype(jnp.float32) / (4.0 * L))


def turn(steps, period):
    angle = (2.0 * jnp.pi / period) * jnp.mod(steps, period).astype(jnp.float32)
    return jnp.cos(angle), jnp.sin(angle)


def gather_kernel(
    n, share, half_ref, sky_ref, alive_ref, vis_ref, count_ref, beam_ref, all_ref, data_ref,
    beam_buf, beam_sem, send1, recv1, send2, recv2,
):
    ma = lax.axis_index("ma")
    pol = lax.axis_index("pol")
    side = lax.rem(pol, 2)
    mate = pol + 1 - 2 * side
    local_m, modes, width = beam_buf.shape

    def beam_copy(i):
        return pltpu.make_async_copy(beam_ref.at[i], beam_buf.at[i], beam_sem.at[i])

    def peer_copy(d):
        return pltpu.make_async_remote_copy(
            src_ref=half_ref.at[side], dst_ref=all_ref.at[side, ma],
            send_sem=send1.at[d], recv_sem=recv1.at[d],
            device_id=(lax.rem(ma + d, n), pol), device_id_type=MESH,
        )

    def mate_copy(d):
        source = lax.rem(ma + n - d, n)
        return pltpu.make_async_remote_copy(
            src_ref=all_ref.at[side, source], dst_ref=all_ref.at[side, source],
            send_sem=send2.at[d], recv_sem=recv2.at[d],
            device_id=(ma, mate), device_id_type=MESH,
        )

    for i in range(local_m):
        beam_copy(i).start()

    barrier = pltpu.get_barrier_semaphore()

    @pl.loop(1, n)
    def _(d):
        pl.semaphore_signal(
            barrier, inc=1, device_id=(lax.rem(ma + d, n), pol), device_id_type=MESH
        )

    pl.semaphore_signal(barrier, inc=1, device_id=(ma, mate), device_id_type=MESH)
    pl.semaphore_wait(barrier, n)

    @pl.loop(1, n)
    def _(d):
        peer_copy(d).start()

    all_ref[0, ma] = half_ref[0]
    all_ref[1, ma] = half_ref[1]

    mode_index = pol * modes + lax.broadcasted_iota(jnp.int32, (modes, 1), 0)

    def one_order(i):
        beam_copy(i).wait()
        mine = lax.broadcasted_iota(jnp.int32, (local_m, 1), 0) == i
        total = jnp.zeros((modes, 128), jnp.float32)
        for t in range(0, width, 128):
            row = sky_ref[i, :, t : t + 128]
            total = total + beam_buf[i, :, t : t + 128].astype(jnp.float32) * row
        image = jnp.sum(total, axis=1, keepdims=True)
        misfit = jnp.where(mode_index < count_ref[i], image - vis_ref[i], 0.0)
        spread = jnp.broadcast_to(
            misfit.astype(jnp.bfloat16).astype(jnp.float32), (modes, 128)
        )
        for t in range(0, width, 128):
            column = jnp.sum(
                beam_buf[i, :, t : t + 128].astype(jnp.float32) * spread, axis=0, keepdims=True
            )
            b, o = t // share, t % share
            data_ref[b, :, o : o + 128] += jnp.where(mine, column, 0.0)

    data_ref[...] = jnp.zeros_like(data_ref)
    early = local_m // 2

    @pl.loop(0, early)
    def _(i):
        one_order(i)

    @pl.loop(1, n)
    def _(d):
        peer_copy(d).wait_recv()
        mate_copy(d).start()

    @pl.loop(early, local_m)
    def _(i):
        one_order(i)

    for b in range(width // share):
        data_ref[b] = data_ref[b] * alive_ref[:, b * share : (b + 1) * share]

    @pl.loop(1, n)
    def _(d):
        peer_copy(d).wait_send()
        mate_copy(d).wait_send()
        mate_copy(d).wait_recv()


def prior_kernel(
    n, local_m, share, sky_ref, kern_ref, cp_ref, sp_ref, order_ref, weight_ref,
    lat_fc, lat_fs, lat_cc, lat_cs, four_fc, four_fs, four_cc, four_cs,
    fort_fc, fort_fs, fort_cc, fort_cs, out_ref,
    tab, four, fort, scaled, synth, total,
):
    scales = kern_ref.shape[0]
    rows = four.shape[0]
    cycles = tab.shape[1]
    amplitude = math.sqrt(2.0 / L)
    norm = 1.0 / math.sqrt(rows // 2)

    @pl.loop(0, tab.shape[0] // FINE_ELL)
    def _(b):
        cc = lat_cc[b] * amplitude
        cs = lat_cs[b] * amplitude
        at = pl.ds(pl.multiple_of(b * FINE_ELL, FINE_ELL), FINE_ELL)
        tab[at, :] = (lat_fc[...] * cc - lat_fs[...] * cs).astype(jnp.bfloat16)

    for b in range(CYCLES // PIX_FINE):
        at = slice(b * PIX_FINE, (b + 1) * PIX_FINE)
        four[:, at] = (
            (four_fc[...] * four_cc[:, b : b + 1] - four_fs[...] * four_cs[:, b : b + 1]) * norm
        ).astype(jnp.bfloat16)
        fort[at, :] = (
            (fort_fc[...] * fort_cc[b : b + 1, :] - fort_fs[...] * fort_cs[b : b + 1, :]) * norm
        ).astype(jnp.bfloat16)

    half = L // 2
    for j in range(scales):
        for h in range(2):
            scaled[j * rows : (j + 1) * rows, h * half : (h + 1) * half] = (
                kern_ref[j : j + 1, h * half : (h + 1) * half] * sky_ref[h].astype(jnp.float32)
            ).astype(jnp.bfloat16)
    for j in range(scales):
        part = scaled[j * rows : (j + 1) * rows, :]
        with_cos = jnp.dot(part, tab[0:L, :], preferred_element_type=jnp.float32)
        with_sin = jnp.dot(part, tab[L : 2 * L, :], preferred_element_type=jnp.float32)
        synth[j * rows : (j + 1) * rows, :] = (
            cp_ref[...] * with_cos - sp_ref[...] * with_sin
        ).astype(jnp.bfloat16)

    total[...] = jnp.zeros_like(total)

    @pl.loop(0, CYCLES // PIX_TILE)
    def _(t):
        at = pl.ds(pl.multiple_of(t * PIX_TILE, PIX_TILE), PIX_TILE)
        left = fort[at, :]
        right = four[:, at]
        for j in range(scales):
            mine = slice(j * rows, (j + 1) * rows)
            pixels = jnp.dot(left, synth[mine, :], preferred_element_type=jnp.float32)
            slopes = (
                weight_ref[...] * pixels * lax.rsqrt(pixels * pixels + smoothing * smoothing)
            ).astype(jnp.bfloat16)
            total[mine, :] += jnp.dot(right, slopes, preferred_element_type=jnp.float32)

    contract_last = (((1,), (1,)), ((), ()))
    for t in range(0, L, share):
        ell = t + lax.broadcasted_iota(jnp.int32, (1, share), 1)
        prior = jnp.zeros((rows, share), jnp.float32)
        for j in range(scales):
            cycle_b = total[j * rows : (j + 1) * rows, :].astype(jnp.bfloat16)
            back_cos = lax.dot_general(
                cycle_b, tab[t : t + share, :], contract_last, preferred_element_type=jnp.float32
            )
            back_sin = lax.dot_general(
                cycle_b, tab[L + t : L + t + share, :], contract_last,
                preferred_element_type=jnp.float32,
            )
            prior = prior + kern_ref[j : j + 1, t : t + share] * (
                cp_ref[...] * back_cos - sp_ref[...] * back_sin
            )
        prior = jnp.where(ell >= order_ref[...], prior_weight * prior, 0.0)
        for d in range(n):
            for c in range(2):
                first = (2 * d + c) * local_m
                piece = prior[first : first + local_m, :]
                out_ref[(c * L + t) // share, d] = jnp.concatenate(
                    [piece[:, : share // 2], piece[:, share // 2 :]], axis=0
                ).astype(jnp.bfloat16)


def reduce_kernel(
    n, pols, prior_ref, data_ref, out_ref, mate_in, sums, peer_in, data_in,
    send_a, recv_a, send_b, recv_b, send_d, recv_d,
):
    ma = lax.axis_index("ma")
    pol = lax.axis_index("pol")
    side = lax.rem(pol, 2)
    mate = pol + 1 - 2 * side
    pairs = pols // 2
    pair = pol // 2
    everyone = n * pairs
    place = ma * pairs + pair
    local_m = out_ref.shape[0]
    share = out_ref.shape[1]

    def data_copy(d):
        other = lax.rem(pol + d, pols)
        return pltpu.make_async_remote_copy(
            src_ref=data_ref.at[other], dst_ref=data_in.at[d - 1],
            send_sem=send_d.at[d - 1], recv_sem=recv_d.at[d - 1],
            device_id=(ma, other), device_id_type=MESH,
        )

    def mate_copy(h):
        return pltpu.make_async_remote_copy(
            src_ref=prior_ref.at[2 * h + 1 - side], dst_ref=mate_in.at[h],
            send_sem=send_a.at[h], recv_sem=recv_a.at[h],
            device_id=(ma, mate), device_id_type=MESH,
        )

    def peer_copy(d):
        target = lax.rem(place + d, everyone)
        target_ma = target // pairs
        target_pair = lax.rem(target, pairs)
        return pltpu.make_async_remote_copy(
            src_ref=sums.at[target_pair, target_ma], dst_ref=peer_in.at[d - 1],
            send_sem=send_b.at[d - 1], recv_sem=recv_b.at[d - 1],
            device_id=(target_ma, 2 * target_pair + side), device_id_type=MESH,
        )

    barrier = pltpu.get_barrier_semaphore()

    @pl.loop(1, everyone)
    def _(d):
        target = lax.rem(place + d, everyone)
        pl.semaphore_signal(
            barrier, inc=1,
            device_id=(target // pairs, 2 * lax.rem(target, pairs) + side), device_id_type=MESH,
        )

    for d in range(1, pols, 2):
        pl.semaphore_signal(
            barrier, inc=1, device_id=(ma, lax.rem(pol + d, pols)), device_id_type=MESH
        )
    pl.semaphore_wait(barrier, everyone - 1 + pairs)

    for h in range(pairs):
        mate_copy(h).start()
    for d in range(1, pols):
        data_copy(d).start()
    for h in range(pairs):
        mate_copy(h).wait_recv()
        sums[h] = (
            prior_ref[2 * h + side].astype(jnp.float32) + mate_in[h].astype(jnp.float32)
        ).astype(jnp.bfloat16)

    @pl.loop(1, everyone)
    def _(d):
        peer_copy(d).start()

    result = data_ref[pol]
    for d in range(1, pols):
        data_copy(d).wait_recv()
        result = result + data_in[d - 1]

    def add(d, running):
        peer_copy(d).wait_recv()
        return running + peer_in[d - 1].astype(jnp.float32)

    prior = lax.fori_loop(1, everyone, add, sums[pair, ma].astype(jnp.float32))
    out_ref[:, : share // 2] = result[:, : share // 2] + prior[:local_m]
    out_ref[:, share // 2 :] = result[:, share // 2 :] + prior[local_m:]

    for h in range(pairs):
        mate_copy(h).wait_send()
    for d in range(1, pols):
        data_copy(d).wait_send()

    @pl.loop(1, everyone)
    def _(d):
        peer_copy(d).wait_send()


def shards(sky_coeffs, visibilities, beam_blocks, mode_counts, order_table, band_limits):
    local_m, width = sky_coeffs.shape
    modes = beam_blocks.shape[1]
    n = lax.axis_size("ma")
    pols = lax.axis_size("pol")
    ma_pos = lax.axis_index("ma")
    pol_pos = lax.axis_index("pol")
    cycles = CYCLES // n
    scales = J // pols
    share = width // pols
    rows = 2 * n * local_m
    vmem = pl.BlockSpec(memory_space=pltpu.VMEM)
    smem = pl.BlockSpec(memory_space=pltpu.SMEM)
    hbm = pl.BlockSpec(memory_space=pl.ANY)
    f32, bf16, i32 = jnp.float32, jnp.bfloat16, jnp.int32
    shape = jax.ShapeDtypeStruct
    sem = pltpu.SemaphoreType.DMA

    local_orders = lax.dynamic_slice_in_dim(order_table, ma_pos * local_m, local_m)
    ell_index = jnp.arange(width, dtype=i32) % L
    alive = ell_index[None, :] >= local_orders[:, None]
    masked = jnp.where(alive, sky_coeffs, jnp.zeros_like(sky_coeffs))
    halves = masked.reshape(local_m, 2, 2, L // 2).transpose(2, 1, 0, 3)
    halves = halves.reshape(2, 2 * local_m, L // 2)
    everything, data = pl.pallas_call(
        functools.partial(gather_kernel, n, share),
        out_shape=(
            shape((2, n, 2 * local_m, L // 2), bf16), shape((pols, local_m, share), f32),
        ),
        in_specs=[vmem, vmem, vmem, vmem, smem, hbm],
        out_specs=(vmem, vmem),
        scratch_shapes=[
            pltpu.VMEM((local_m, modes, width), bf16), sem((local_m,)),
            sem((n,)), sem((n,)), sem((n,)), sem((n,)),
        ],
        compiler_params=pltpu.CompilerParams(
            collective_id=0, has_side_effects=True, vmem_limit_bytes=40 * 2**20
        ),
    )(
        halves, masked.astype(f32)[:, None, :], alive.astype(f32), visibilities.astype(f32)[:, :, None],
        mode_counts, beam_blocks,
    )

    my_limits = lax.dynamic_slice_in_dim(band_limits, pol_pos * scales, scales, 0)
    kernel_rows = band_kernel(my_limits)
    row_orders = jnp.broadcast_to(order_table.reshape(n, 1, local_m), (n, 2, local_m)).reshape(rows)
    row_part = jnp.broadcast_to(
        jnp.arange(2, dtype=i32)[None, :, None], (n, 2, local_m)
    ).reshape(rows)
    cos_phase, sin_phase = order_phases(row_orders)
    weights = cycle_weights(ma_pos * cycles, cycles)
    period = 8 * CYCLES
    cycle_odd = 2 * (ma_pos * cycles + jnp.arange(cycles, dtype=i32))[None, :] + 1
    fine = 2 * jnp.arange(FINE_ELL, dtype=i32)[:, None] + 1
    coarse = 2 * FINE_ELL * jnp.arange(L // FINE_ELL, dtype=i32)[:, None]
    coarse_steps = coarse * cycle_odd - CYCLES
    lat_fine = turn(fine * cycle_odd, period)
    lat_coarse = turn(jnp.concatenate([coarse_steps, coarse_steps - period // 4]), period)
    lat_coarse = [table[:, None, :] for table in lat_coarse]
    pix_fine = jnp.arange(PIX_FINE, dtype=i32)
    pix_coarse = PIX_FINE * jnp.arange(CYCLES // PIX_FINE, dtype=i32)
    four_fine = turn(row_orders[:, None] * pix_fine[None, :], CYCLES)
    four_coarse = turn(
        row_orders[:, None] * pix_coarse[None, :] + (CYCLES // 4) * row_part[:, None], CYCLES
    )
    fort_fine = turn(row_orders[None, :] * pix_fine[:, None], CYCLES)
    fort_coarse = turn(
        row_orders[None, :] * pix_coarse[:, None] + (CYCLES // 4) * row_part[None, :], CYCLES
    )
    prior = pl.pallas_call(
        functools.partial(prior_kernel, n, local_m, share),
        out_shape=shape((pols, n, 2 * local_m, share // 2), bf16),
        in_specs=[vmem] * 18,
        out_specs=vmem,
        scratch_shapes=[
            pltpu.VMEM((2 * L, cycles), bf16),
            pltpu.VMEM((rows, CYCLES), bf16),
            pltpu.VMEM((CYCLES, rows), bf16),
            pltpu.VMEM((scales * rows, L), bf16),
            pltpu.VMEM((scales * rows, cycles), bf16),
            pltpu.VMEM((scales * rows, cycles), f32),
        ],
        compiler_params=pltpu.CompilerParams(vmem_limit_bytes=56 * 2**20),
    )(
        everything.reshape(2, rows, L // 2), kernel_rows, cos_phase[:, None], sin_phase[:, None],
        row_orders[:, None], weights[None, :],
        *lat_fine, *lat_coarse, *four_fine, *four_coarse, *fort_fine, *fort_coarse,
    )

    everyone = n * (pols // 2)
    piece = (2 * local_m, share // 2)
    return pl.pallas_call(
        functools.partial(reduce_kernel, n, pols),
        out_shape=shape((local_m, share), f32),
        in_specs=[vmem, vmem],
        out_specs=vmem,
        scratch_shapes=[
            pltpu.VMEM((pols // 2, n) + piece, bf16),
            pltpu.VMEM((pols // 2, n) + piece, bf16),
            pltpu.VMEM((everyone - 1,) + piece, bf16),
            pltpu.VMEM((pols - 1, local_m, share), f32),
            sem((pols // 2,)), sem((pols // 2,)),
            sem((everyone - 1,)), sem((everyone - 1,)),
            sem((pols - 1,)), sem((pols - 1,)),
        ],
        compiler_params=pltpu.CompilerParams(
            collective_id=1, has_side_effects=True, vmem_limit_bytes=40 * 2**20
        ),
    )(prior, data)


def solution(mesh):
    placed = (P("ma", None), P("ma", "pol"), P("ma", "pol", None), P("ma"), P(), P())
    return jax.shard_map(
        shards, mesh=mesh, in_specs=placed, out_specs=P("ma", "pol"), check_vma=False
    )
```

profile of v0, /device:TPU:0, one launch (start us, length us, event | category | flops | bytes accessed | tf_op | source)
XLA Modules:
  0.0 66.9 jit_solution(11639014305562655087)
XLA Ops:
  0.0 0.8 %dynamic_slice.6 = s32[8]{0:T(128)S(1)} dynamic-slice(s32[64]{0:T(128)} %param.10, s32[]{:T(128)S(6)} %select_n.88), dynamic_slice_sizes={8} | dynamic-slice | bytes 68 | tf_op jit(solution)/shard_map/dynamic_slice | solution.py:341
  0.8 0.9 %bitcast_convert_fusion = (f32[8,1,4096]{2,0,1:T(8,128)S(1)}, bf16[8,4096]{1,0:T(8,128)(2,1)S(1)}) fusion(bf16[8,4096]{1,0:T(8,128)(2,1)} %param.6, s32[8]{0:T(128)S(1)} %dynamic_slice.6, s32[4096]{0:T(1024)S(1)} %add_select_fusion.7), kind=kLoop, calls=%fused_computation.36 | loop fusion | flops 98304 | bytes 278560 | tf_op jit(solution)/shard_map/broadcast_in_dim | solution.py:362
  1.7 0.1 copy.23.sky_ref
  1.9 0.1 compare_convert_fusion.alive_ref
  2.0 0.7 %bitcast_convert_fusion.1 = f32[8,128,1]{1,0,2:T(8,128)S(1)} fusion(bf16[8,128]{1,0:T(8,128)(2,1)} %param.7), kind=kLoop, calls=%fused_computation.76 | loop fusion | flops 1024 | bytes 6144 | tf_op jit(solution)/shard_map/broadcast_in_dim | solution.py:362
  2.7 0.2 copy.24.vis_ref
  2.9 0.0 copy-start.1
  2.9 3.4 %copy-done.1 = bf16[8,128,4096]{2,1,0:T(8,128)(2,1)S(1)} copy-done((bf16[8,128,4096]{2,1,0:T(8,128)(2,1)S(1)}, bf16[8,128,4096]{2,1,0:T(8,128)(2,1)}, u32[]{:S(2)}) %copy-start.1) | copy-done | bytes 8388632
  6.3 0.7 copy-done.4
  6.9 15.0 %shard_map.64 = (bf16[2,8,16,1024]{3,2,1,0:T(8,128)(2,1)S(1)}, f32[4,8,1024]{2,1,0:T(8,128)S(1)}) custom-call(bf16[2,16,1024]{2,1,0:T(8,128)(2,1)S(1)} %bitcast.24, f32[8,1,4096]{2,1,0:T(1,128)S(1)} %copy.23.sky_ref, f32[8,4096]{1,0:T(8,128)S(1)} %compare_convert_fusion.alive_ref, f32[8,128,1]{2,1,0:T(8,128)S(1)} %copy.24.vis_ref, s32[8]{0:T(128)S(1)} %copy-done.4, ...), custom_call_target="tpu_custom_call" | custom-call | tf_op jit(solution)/shard_map/pallas_call | solution.py:347
  21.9 0.8 %copy-done.3 = bf16[2,8,16,1024]{3,2,1,0:T(8,128)(2,1)} copy-done((bf16[2,8,16,1024]{3,2,1,0:T(8,128)(2,1)}, bf16[2,8,16,1024]{3,2,1,0:T(8,128)(2,1)S(1)}, u32[]{:S(2)}) %copy-start.3) | copy-done | bytes 524312
  22.7 0.1 constant_dynamic-slice_fusion
  22.8 0.9 %and_select_fusion.kern_ref = f32[2,2048]{1,0:T(2,128)} fusion(f32[2]{0:T(128)S(1)} %get-tuple-element.24, s32[2]{0:T(128)S(1)} %get-tuple-element.25, s32[2]{0:T(128)S(1)} %get-tuple-element.23), kind=kLoop, calls=%fused_computation.54 | loop fusion | flops 36864 | bytes 16408 | tf_op jit(solution)/shard_map/jit(_where)/select_n | solution.py:38
  23.7 0.1 fusion.2
  23.8 0.1 fusion.1
  24.0 8.2 %fusion.34 = (f32[128,1,512]{2,1,0:T(1,128)}, f32[128,1,512]{2,1,0:T(1,128)}) fusion(f32[128,1,512]{2,0,1:T(8,128)S(1)} %fusion.1), kind=kLoop, calls=%fused_computation.71 | loop fusion | flops 65536 | bytes 786432 | tf_op jit(solution)/shard_map/sin | solution.py:48
  32.1 0.1 broadcast_in_dim.53
  32.2 0.1 mul.273
  32.3 1.3 %fusion.20 = (f32[128,128]{1,0:T(8,128)}, f32[128,128]{1,0:T(8,128)}, f32[128,128]{1,0:T(8,128)}, f32[128,128]{1,0:T(8,128)}) fusion(s32[128]{0:T(128)S(1)} %mul.273), kind=kLoop, calls=%fused_computation.48 | loop fusion | flops 458752 | bytes 262656 | tf_op jit(solution)/shard_map/sin | solution.py:48
  33.6 0.1 mul.285
  33.7 0.1 fusion.27
  33.8 0.1 copy.29
  33.9 0.9 %multiply_sine_fusion = (f32[128,32]{1,0:T(8,128)}, f32[128,32]{1,0:T(8,128)}) fusion(f32[128,32]{1,0:T(8,128)S(1)} %copy.29), kind=kLoop, calls=%fused_computation.46 | loop fusion | flops 4096 | bytes 49152 | tf_op jit(solution)/shard_map/sin | solution.py:48
  34.8 0.8 %fusion.36 = (f32[32,128]{1,0:T(8,128)}, f32[32,128]{1,0:T(8,128)}) fusion(s32[128]{0:T(128)S(1)} %mul.285, s32[32]{0:T(128)S(1)} %iota_multiply_fusion.1, s32[128]{0:T(128)S(1)} %mul.273), kind=kLoop, calls=%fused_computation.73 | loop fusion | flops 61440 | bytes 33920 | tf_op jit(solution)/shard_map/sin | solution.py:48
  35.6 1.0 %fusion.24 = (f32[32,512]{1,0:T(8,128)}, f32[32,512]{1,0:T(8,128)}) fusion(s32[512]{0:T(512)S(1)} %multiply_add_fusion.2, s32[32]{0:T(128)S(1)} %multiply_add_fusion.3), kind=kLoop, calls=%fused_computation.52 | loop fusion | flops 229376 | bytes 133248 | tf_op jit(solution)/shard_map/sin | solution.py:48
  36.6 0.1 reshape.421.order_ref
  36.7 0.7 %convert_subtract_fusion = (f32[128,1]{1,0:T(8,128)}, f32[128,1]{1,0:T(8,128)}) fusion(s32[128,1]{1,0:T(8,128)S(1)} %reshape.421.order_ref), kind=kLoop, calls=%fused_computation.42 | loop fusion | flops 2688 | bytes 1536 | tf_op jit(solution)/shard_map/sub | solution.py:26
  37.4 0.7 %multiply_sine_fusion.1.weight_ref = f32[1,512]{1,0:T(1,128)} fusion(s32[]{:T(128)S(6)} %mul.254), kind=kLoop, calls=%fused_computation.78 | loop fusion | flops 2560 | bytes 2052 | tf_op jit(solution)/shard_map/sin | solution.py:43
  38.0 15.8 %shard_map.65.prior_ref = bf16[4,8,16,512]{3,2,1,0:T(8,128)(2,1)} custom-call(bf16[2,128,1024]{2,1,0:T(8,128)(2,1)} %bitcast.23, f32[2,2048]{1,0:T(2,128)} %and_select_fusion.kern_ref, f32[128,1]{1,0:T(8,128)} %get-tuple-element.16.cp_ref, f32[128,1]{1,0:T(8,128)} %get-tuple-element.15.sp_ref, s32[128,1]{1,0:T(8,128)} %copy-done.5, ...), custom_call_target="tpu_custom_call" | custom-call | tf_op jit(solution)/shard_map/pallas_call | solution.py:392
  53.8 1.0 %copy-done.2 = bf16[4,8,16,512]{3,2,1,0:T(8,128)(2,1)S(1)} copy-done((bf16[4,8,16,512]{3,2,1,0:T(8,128)(2,1)S(1)}, bf16[4,8,16,512]{3,2,1,0:T(8,128)(2,1)}, u32[]{:S(2)}) %copy-start.2) | copy-done | bytes 524312
  54.8 11.5 %shard_map.66 = f32[8,1024]{1,0:T(8,128)S(1)} custom-call(bf16[4,8,16,512]{3,2,1,0:T(8,128)(2,1)S(1)} %copy-done.2, f32[4,8,1024]{2,1,0:T(8,128)S(1)} %get-tuple-element.8.data_ref), custom_call_target="tpu_custom_call" | custom-call | tf_op jit(solution)/shard_map/pallas_call | solution.py:414
  66.3 0.6 copy.39
  (18 shorter events, 0.1 us)
Async XLA Ops:
  0.0 22.7 %copy-start = (s32[8,2]{0,1:T(2,128)S(1)}, s32[8,2]{0,1:T(2,128)}, u32[]{:S(2)}) copy-start(s32[8,2]{0,1:T(2,128)} %param.11) | copy-start | bytes 196
  0.0 32.1 %copy-start.6 = (s32[64]{0:T(128)S(1)}, s32[64]{0:T(128)}, u32[]{:S(2)}) copy-start(s32[64]{0:T(128)} %param.10) | copy-start | bytes 772
  2.9 3.4 %copy-start.1 = (bf16[8,128,4096]{2,1,0:T(8,128)(2,1)S(1)}, bf16[8,128,4096]{2,1,0:T(8,128)(2,1)}, u32[]{:S(2)}) copy-start(bf16[8,128,4096]{2,1,0:T(8,128)(2,1)} %beam_ref.1) | copy-start | bytes 25165828
  6.3 0.7 copy-start.4
  21.9 0.8 %copy-start.3 = (bf16[2,8,16,1024]{3,2,1,0:T(8,128)(2,1)}, bf16[2,8,16,1024]{3,2,1,0:T(8,128)(2,1)S(1)}, u32[]{:S(2)}) copy-start(bf16[2,8,16,1024]{3,2,1,0:T(8,128)(2,1)S(1)} %get-tuple-element.7) | copy-start | bytes 1572868
  36.6 1.4 %copy-start.5 = (s32[128,1]{1,0:T(8,128)}, s32[128,1]{1,0:T(8,128)S(1)}, u32[]{:S(2)}) copy-start(s32[128,1]{1,0:T(8,128)S(1)} %reshape.421.order_ref) | copy-start | bytes 1540
  53.8 1.0 %copy-start.2 = (bf16[4,8,16,512]{3,2,1,0:T(8,128)(2,1)S(1)}, bf16[4,8,16,512]{3,2,1,0:T(8,128)(2,1)}, u32[]{:S(2)}) copy-start(bf16[4,8,16,512]{3,2,1,0:T(8,128)(2,1)} %shard_map.65.prior_ref) | copy-start | bytes 1572868
where the time goes:
time: 67.7 us; the launch traced here: 66.9 us
  Pallas kernels  42.2 us (62%)
  other arithmetic  16.4 us (24%)
  local copies, waits for them, and re-layouts  8.18 us (12%)
    pallas_call x1, Pallas kernels, shards(): pl.pallas_call(functools.partial(prior_kernel, n, local_m, share), out_sh...  15.8 us
    pallas_call x1, Pallas kernels, shards(): pl.pallas_call(functools.partial(gather_kernel, n, share), out_shape=(sha...  15 us
    sin x5, other arithmetic, turn(): return (jnp.cos(angle), jnp.sin(angle))  12.1 us
    pallas_call x1, Pallas kernels, shards(): pl.pallas_call(functools.partial(reduce_kernel, n, pols), out_shape=shape...  11.5 us
    unnamed x15, local copies, waits for them, and re-layouts  6.49 us

commit v1 on v0

v1 whole, which is shorter than its diff:
```python
import functools
import math

import jax
import jax.numpy as jnp
from jax import lax
from jax.experimental import pallas as pl
from jax.experimental.pallas import tpu as pltpu
from jax.sharding import PartitionSpec as P

L = 2048
J = 8
CYCLES = 2 * L
FINE_ELL = 32
PIX_FINE = 128
PIX_TILE = 512
MESH = pl.DeviceIdType.MESH

smoothing = 0.1
prior_weight = 0.2


def short_waves(angle):
    z = angle * angle
    sine = angle * (1.0 + z * (-1.0 / 6 + z * (1.0 / 120 + z * (-1.0 / 5040 + z / 362880.0))))
    cosine = 1.0 + z * (
        -0.5 + z * (1.0 / 24 + z * (-1.0 / 720 + z * (1.0 / 40320 - z / 3628800.0)))
    )
    return cosine, sine


def turn(steps, period):
    centred = jnp.bitwise_and(steps, period - 1) - period // 2
    cosine, sine = short_waves(centred.astype(jnp.float32) * (0.5 * math.pi / period))
    cosine, sine = 1.0 - 2.0 * sine * sine, 2.0 * sine * cosine
    return 2.0 * sine * sine - 1.0, -2.0 * sine * cosine


def band_row(low, high):
    ell = lax.broadcasted_iota(jnp.int32, (1, L), 1)
    span = jnp.full((1, L), high - low, jnp.int32).astype(jnp.float32)
    fraction = (ell - low).astype(jnp.float32) / span
    inside = (ell >= low) & (ell <= high)
    cosine, sine = short_waves(0.5 * math.pi * (jnp.where(inside, fraction, 0.5) - 0.5))
    return jnp.where(inside, (1.0 - 2.0 * sine * sine) ** 2, 0.0)


def gather_kernel(
    n, share, sky_ref, order_ref, vis_ref, count_ref, beam_ref, all_ref, data_ref,
    sky_rows, vis_rows, beam_buf, beam_sem, send1, recv1, send2, recv2,
):
    ma = lax.axis_index("ma")
    pol = lax.axis_index("pol")
    side = lax.rem(pol, 2)
    mate = pol + 1 - 2 * side
    local_m, modes, width = beam_buf.shape

    def beam_copy(i):
        return pltpu.make_async_copy(beam_ref.at[i], beam_buf.at[i], beam_sem.at[i])

    def peer_copy(d):
        return pltpu.make_async_remote_copy(
            src_ref=all_ref.at[side, ma], dst_ref=all_ref.at[side, ma],
            send_sem=send1.at[d], recv_sem=recv1.at[d],
            device_id=(lax.rem(ma + d, n), pol), device_id_type=MESH,
        )

    def mate_copy(d):
        source = lax.rem(ma + n - d, n)
        return pltpu.make_async_remote_copy(
            src_ref=all_ref.at[side, source], dst_ref=all_ref.at[side, source],
            send_sem=send2.at[d], recv_sem=recv2.at[d],
            device_id=(ma, mate), device_id_type=MESH,
        )

    for i in range(local_m):
        beam_copy(i).start()

    orders = order_ref[pl.ds(pl.multiple_of(ma * local_m, local_m), local_m), :]
    alive = lax.rem(lax.broadcasted_iota(jnp.int32, (1, width), 1), L) >= orders
    masked = jnp.where(alive, sky_ref[...].astype(jnp.float32), 0.0)
    half = L // 2
    for h in range(2):
        all_ref[h, ma] = jnp.concatenate(
            [masked[:, h * half : (h + 1) * half], masked[:, L + h * half : L + (h + 1) * half]],
            axis=0,
        ).astype(jnp.bfloat16)
    vis = vis_ref[...].astype(jnp.float32)
    for i in range(local_m):
        sky_rows[i] = masked[i : i + 1]
        vis_rows[i] = vis[i : i + 1]

    barrier = pltpu.get_barrier_semaphore()

    @pl.loop(1, n)
    def _(d):
        pl.semaphore_signal(
            barrier, inc=1, device_id=(lax.rem(ma + d, n), pol), device_id_type=MESH
        )

    pl.semaphore_signal(barrier, inc=1, device_id=(ma, mate), device_id_type=MESH)
    pl.semaphore_wait(barrier, n)

    @pl.loop(1, n)
    def _(d):
        peer_copy(d).start()

    mode_index = pol * modes + lax.broadcasted_iota(jnp.int32, (modes, 1), 0)
    diagonal = lax.broadcasted_iota(jnp.int32, (modes, modes), 0) == lax.broadcasted_iota(
        jnp.int32, (modes, modes), 1
    )

    def one_order(i):
        beam_copy(i).wait()
        mine = lax.broadcasted_iota(jnp.int32, (local_m, 1), 0) == i
        total = jnp.where(diagonal, -vis_rows[i], 0.0)
        for t in range(0, width, 128):
            row = sky_rows[i, :, t : t + 128]
            total = total + beam_buf[i, :, t : t + 128].astype(jnp.float32) * row
        image = jnp.sum(total, axis=1, keepdims=True)
        misfit = jnp.where(mode_index < count_ref[i], image, 0.0)
        spread = jnp.broadcast_to(
            misfit.astype(jnp.bfloat16).astype(jnp.float32), (modes, 128)
        )
        for t in range(0, width, 128):
            column = jnp.sum(
                beam_buf[i, :, t : t + 128].astype(jnp.float32) * spread, axis=0, keepdims=True
            )
            b, o = t // share, t % share
            data_ref[b, :, o : o + 128] += jnp.where(mine, column, 0.0)

    data_ref[...] = jnp.zeros_like(data_ref)
    early = local_m // 2

    @pl.loop(0, early)
    def _(i):
        one_order(i)

    @pl.loop(1, n)
    def _(d):
        peer_copy(d).wait_recv()
        mate_copy(d).start()

    @pl.loop(early, local_m)
    def _(i):
        one_order(i)

    for b in range(width // share):
        ell = lax.rem(b * share + lax.broadcasted_iota(jnp.int32, (1, share), 1), L)
        data_ref[b] = jnp.where(ell >= orders, data_ref[b], 0.0)

    @pl.loop(1, n)
    def _(d):
        peer_copy(d).wait_send()
        mate_copy(d).wait_send()
        mate_copy(d).wait_recv()


def prior_kernel(
    n, local_m, share, sky_ref, limit_ref, order_ref, turned_ref, out_ref,
    tab, four, fort, coarse_cos, coarse_sin, scaled, synth, total,
):
    ma = lax.axis_index("ma")
    pol = lax.axis_index("pol")
    rows = four.shape[0]
    cycles = tab.shape[1]
    scales = synth.shape[0] // rows
    amplitude = math.sqrt(2.0 / L)
    norm = 1.0 / math.sqrt(rows // 2)

    def index(count, axis):
        return lax.broadcasted_iota(jnp.int32, (count, 1) if axis == 0 else (1, count), axis)

    kern = [
        band_row(limit_ref[pol * scales + j, 0], limit_ref[pol * scales + j, 1])
        for j in range(scales)
    ]
    quarter = jnp.bitwise_and(order_ref[...], 3)
    cp = jnp.where(quarter == 0, 1.0, jnp.where(quarter == 2, -1.0, 0.0))
    sp = jnp.where(quarter == 1, 1.0, jnp.where(quarter == 3, -1.0, 0.0))
    odd = 2 * (ma * cycles + index(cycles, 1)) + 1
    _, weight = turn(odd, 4 * CYCLES)

    period = 8 * CYCLES
    blocks = L // FINE_ELL
    coarse = 2 * FINE_ELL * index(blocks, 0) * odd - CYCLES
    for part in range(2):
        cosine, sine = turn(coarse - part * (period // 4), period)
        for b in range(blocks):
            coarse_cos[part * blocks + b] = amplitude * cosine[b : b + 1]
            coarse_sin[part * blocks + b] = amplitude * sine[b : b + 1]
    fine_cos, fine_sin = turn((2 * index(FINE_ELL, 0) + 1) * odd, period)

    @pl.loop(0, 2 * blocks)
    def _(b):
        at = pl.ds(pl.multiple_of(b * FINE_ELL, FINE_ELL), FINE_ELL)
        tab[at, :] = (fine_cos * coarse_cos[b] - fine_sin * coarse_sin[b]).astype(jnp.bfloat16)

    steps = CYCLES // PIX_FINE
    down, across = order_ref[...], turned_ref[...]
    quarter_turn = CYCLES // 4
    down_part = lax.rem(index(rows, 0) // local_m, 2) * quarter_turn
    across_part = lax.rem(index(rows, 1) // local_m, 2) * quarter_turn
    down_fine = turn(down * index(PIX_FINE, 1), CYCLES)
    down_coarse = turn(down * (PIX_FINE * index(steps, 1)) + down_part, CYCLES)
    across_fine = turn(across * index(PIX_FINE, 0), CYCLES)
    across_coarse = turn(across * (PIX_FINE * index(steps, 0)) + across_part, CYCLES)
    down_fine = [norm * part for part in down_fine]
    across_fine = [norm * part for part in across_fine]
    for b in range(steps):
        at = slice(b * PIX_FINE, (b + 1) * PIX_FINE)
        four[:, at] = (
            down_fine[0] * down_coarse[0][:, b : b + 1]
            - down_fine[1] * down_coarse[1][:, b : b + 1]
        ).astype(jnp.bfloat16)
        fort[at, :] = (
            across_fine[0] * across_coarse[0][b : b + 1, :]
            - across_fine[1] * across_coarse[1][b : b + 1, :]
        ).astype(jnp.bfloat16)

    half = L // 2
    for j in range(scales):
        for h in range(2):
            scaled[j * rows : (j + 1) * rows, h * half : (h + 1) * half] = (
                kern[j][:, h * half : (h + 1) * half] * sky_ref[h].astype(jnp.float32)
            ).astype(jnp.bfloat16)
    for j in range(scales):
        part = scaled[j * rows : (j + 1) * rows, :]
        with_cos = jnp.dot(part, tab[0:L, :], preferred_element_type=jnp.float32)
        with_sin = jnp.dot(part, tab[L : 2 * L, :], preferred_element_type=jnp.float32)
        synth[j * rows : (j + 1) * rows, :] = (
            cp * with_cos - sp * with_sin
        ).astype(jnp.bfloat16)

    total[...] = jnp.zeros_like(total)

    @pl.loop(0, CYCLES // PIX_TILE)
    def _(t):
        at = pl.ds(pl.multiple_of(t * PIX_TILE, PIX_TILE), PIX_TILE)
        left = fort[at, :]
        right = four[:, at]
        for j in range(scales):
            mine = slice(j * rows, (j + 1) * rows)
            pixels = jnp.dot(left, synth[mine, :], preferred_element_type=jnp.float32)
            slopes = (
                weight * pixels * lax.rsqrt(pixels * pixels + smoothing * smoothing)
            ).astype(jnp.bfloat16)
            total[mine, :] += jnp.dot(right, slopes, preferred_element_type=jnp.float32)

    contract_last = (((1,), (1,)), ((), ()))
    for t in range(0, L, share):
        ell = t + lax.broadcasted_iota(jnp.int32, (1, share), 1)
        prior = jnp.zeros((rows, share), jnp.float32)
        for j in range(scales):
            cycle_b = total[j * rows : (j + 1) * rows, :].astype(jnp.bfloat16)
            back_cos = lax.dot_general(
                cycle_b, tab[t : t + share, :], contract_last, preferred_element_type=jnp.float32
            )
            back_sin = lax.dot_general(
                cycle_b, tab[L + t : L + t + share, :], contract_last,
                preferred_element_type=jnp.float32,
            )
            prior = prior + kern[j][:, t : t + share] * (
                cp * back_cos - sp * back_sin
            )
        prior = jnp.where(ell >= order_ref[...], prior_weight * prior, 0.0)
        for d in range(n):
            for c in range(2):
                first = (2 * d + c) * local_m
                piece = prior[first : first + local_m, :]
                out_ref[(c * L + t) // share, d] = piece


def reduce_kernel(
    n, pols, prior_ref, data_ref, out_ref, mate_in, sums, peer_in, data_in,
    send_a, recv_a, send_b, recv_b, send_d, recv_d,
):
    ma = lax.axis_index("ma")
    pol = lax.axis_index("pol")
    side = lax.rem(pol, 2)
    mate = pol + 1 - 2 * side
    pairs = pols // 2
    pair = pol // 2
    everyone = n * pairs
    place = ma * pairs + pair
    local_m = out_ref.shape[0]
    share = out_ref.shape[1]

    def data_copy(d):
        other = lax.rem(pol + d, pols)
        return pltpu.make_async_remote_copy(
            src_ref=data_ref.at[other], dst_ref=data_in.at[d - 1],
            send_sem=send_d.at[d - 1], recv_sem=recv_d.at[d - 1],
            device_id=(ma, other), device_id_type=MESH,
        )

    def mate_copy(h):
        return pltpu.make_async_remote_copy(
            src_ref=prior_ref.at[2 * h + 1 - side], dst_ref=mate_in.at[h],
            send_sem=send_a.at[h], recv_sem=recv_a.at[h],
            device_id=(ma, mate), device_id_type=MESH,
        )

    def peer_copy(d):
        target = lax.rem(place + d, everyone)
        target_ma = target // pairs
        target_pair = lax.rem(target, pairs)
        return pltpu.make_async_remote_copy(
            src_ref=sums.at[target_pair, target_ma], dst_ref=peer_in.at[d - 1],
            send_sem=send_b.at[d - 1], recv_sem=recv_b.at[d - 1],
            device_id=(target_ma, 2 * target_pair + side), device_id_type=MESH,
        )

    barrier = pltpu.get_barrier_semaphore()

    @pl.loop(1, everyone)
    def _(d):
        target = lax.rem(place + d, everyone)
        pl.semaphore_signal(
            barrier, inc=1,
            device_id=(target // pairs, 2 * lax.rem(target, pairs) + side), device_id_type=MESH,
        )

    for d in range(1, pols, 2):
        pl.semaphore_signal(
            barrier, inc=1, device_id=(ma, lax.rem(pol + d, pols)), device_id_type=MESH
        )
    pl.semaphore_wait(barrier, everyone - 1 + pairs)

    for h in range(pairs):
        mate_copy(h).start()
    for d in range(1, pols):
        data_copy(d).start()
    for h in range(pairs):
        mate_copy(h).wait_recv()
        both = prior_ref[2 * h + side] + mate_in[h]
        sums[h] = jnp.concatenate(
            [both[:, :, : share // 2], both[:, :, share // 2 :]], axis=1
        ).astype(jnp.bfloat16)

    @pl.loop(1, everyone)
    def _(d):
        peer_copy(d).start()

    result = data_ref[pol] + (prior_ref[pol, ma] + mate_in[pair, ma])
    for d in range(1, pols):
        data_copy(d).wait_recv()
        result = result + data_in[d - 1]

    def add(d, running):
        peer_copy(d).wait_recv()
        return running + peer_in[d - 1].astype(jnp.float32)

    prior = lax.fori_loop(1, everyone, add, jnp.zeros(peer_in.shape[1:], jnp.float32))
    out_ref[:, : share // 2] = result[:, : share // 2] + prior[:local_m]
    out_ref[:, share // 2 :] = result[:, share // 2 :] + prior[local_m:]

    for h in range(pairs):
        mate_copy(h).wait_send()
    for d in range(1, pols):
        data_copy(d).wait_send()

    @pl.loop(1, everyone)
    def _(d):
        peer_copy(d).wait_send()


def shards(sky_coeffs, visibilities, beam_blocks, mode_counts, order_table, band_limits):
    local_m, width = sky_coeffs.shape
    modes = beam_blocks.shape[1]
    n = lax.axis_size("ma")
    pols = lax.axis_size("pol")
    cycles = CYCLES // n
    scales = J // pols
    share = width // pols
    rows = 2 * n * local_m
    vmem = pl.BlockSpec(memory_space=pltpu.VMEM)
    smem = pl.BlockSpec(memory_space=pltpu.SMEM)
    hbm = pl.BlockSpec(memory_space=pl.ANY)
    f32, bf16 = jnp.float32, jnp.bfloat16
    shape = jax.ShapeDtypeStruct
    sem = pltpu.SemaphoreType.DMA

    everything, data = pl.pallas_call(
        functools.partial(gather_kernel, n, share),
        out_shape=(
            shape((2, n, 2 * local_m, L // 2), bf16), shape((pols, local_m, share), f32),
        ),
        in_specs=[vmem, vmem, vmem, smem, hbm],
        out_specs=(vmem, vmem),
        scratch_shapes=[
            pltpu.VMEM((local_m, 1, width), f32), pltpu.VMEM((local_m, 1, modes), f32),
            pltpu.VMEM((local_m, modes, width), bf16), sem((local_m,)),
            sem((n,)), sem((n,)), sem((n,)), sem((n,)),
        ],
        compiler_params=pltpu.CompilerParams(
            collective_id=0, has_side_effects=True, vmem_limit_bytes=40 * 2**20
        ),
    )(
        sky_coeffs, order_table[:, None], visibilities, mode_counts, beam_blocks
    )

    row_orders = jnp.broadcast_to(order_table.reshape(n, 1, local_m), (n, 2, local_m)).reshape(rows)
    prior = pl.pallas_call(
        functools.partial(prior_kernel, n, local_m, share),
        out_shape=shape((pols, n, local_m, share), f32),
        in_specs=[vmem, smem, vmem, vmem],
        out_specs=vmem,
        scratch_shapes=[
            pltpu.VMEM((2 * L, cycles), bf16),
            pltpu.VMEM((rows, CYCLES), bf16),
            pltpu.VMEM((CYCLES, rows), bf16),
            pltpu.VMEM((2 * L // FINE_ELL, 1, cycles), f32),
            pltpu.VMEM((2 * L // FINE_ELL, 1, cycles), f32),
            pltpu.VMEM((scales * rows, L), bf16),
            pltpu.VMEM((scales * rows, cycles), bf16),
            pltpu.VMEM((scales * rows, cycles), f32),
        ],
        compiler_params=pltpu.CompilerParams(vmem_limit_bytes=56 * 2**20),
    )(
        everything.reshape(2, rows, L // 2), band_limits, row_orders[:, None], row_orders[None, :]
    )

    everyone = n * (pols // 2)
    piece = (2 * local_m, share // 2)
    return pl.pallas_call(
        functools.partial(reduce_kernel, n, pols),
        out_shape=shape((local_m, share), f32),
        in_specs=[vmem, vmem],
        out_specs=vmem,
        scratch_shapes=[
            pltpu.VMEM((pols // 2, n, local_m, share), f32),
            pltpu.VMEM((pols // 2, n) + piece, bf16),
            pltpu.VMEM((everyone - 1,) + piece, bf16),
            pltpu.VMEM((pols - 1, local_m, share), f32),
            sem((pols // 2,)), sem((pols // 2,)),
            sem((everyone - 1,)), sem((everyone - 1,)),
            sem((pols - 1,)), sem((pols - 1,)),
        ],
        compiler_params=pltpu.CompilerParams(
            collective_id=1, has_side_effects=True, vmem_limit_bytes=40 * 2**20
        ),
    )(prior, data)


def solution(mesh):
    placed = (P("ma", None), P("ma", "pol"), P("ma", "pol", None), P("ma"), P(), P())
    return jax.shard_map(
        shards, mesh=mesh, in_specs=placed, out_specs=P("ma", "pol"), check_vma=False
    )
```

time: 67.7 us -> 56.4 us (0.83)
  other arithmetic: 16.4 us -> 0 us
  local copies, waits for them, and re-layouts: 8.18 us -> 12.3 us
  Pallas kernels: 42.2 us -> 42.9 us
    sin x6 -> x0, other arithmetic: 12.8 us -> none  [the longest x5 12.1 us: turn(): return (jnp.cos(angle), jnp.sin(angle))]
    unnamed x15 -> x14, local copies, waits for them, and re-layouts: 6.49 us -> 9.54 us
    broadcast_in_dim x2 -> x0, other arithmetic: 1.61 us -> none  [the longest x1 0.92 us: shards(): masked.astype(f32)[:, None, :]]
    another operation x0 -> x2, local copies, waits for them, and re-layouts: none -> 1.29 us  [the longest x1 0.71 us: shards(): row_orders[:, None]]
    pallas_call x1, Pallas kernels: 15.8 us -> 16.7 us  [shards(): pl.pallas_call(functools.partial(prior_kernel, n, local_m, share), out_sh...]
    select_n x2 -> x0, other arithmetic: 0.93 us -> none  [the longest x1 0.93 us: band_kernel(): return jnp.where(inside, jnp.sin(jnp.pi * fraction) ** 2, 0.0)]
    dynamic_slice x2 -> x0, local copies, waits for them, and re-layouts: 0.87 us -> none  [the longest x1 0.8 us: shards(): lax.dynamic_slice_in_dim(order_table, ma_pos * local_m, local_m)]
    sub x1 -> x0, other arithmetic: 0.7 us -> none  [order_phases(): (quarter == 1).astype(jnp.float32) - (quarter == 3).astype(jnp.float32)]
where the time goes in v1:
time: 56.4 us; the launch traced here: 55.3 us
  Pallas kernels  42.9 us (76%)
  local copies, waits for them, and re-layouts  12.3 us (22%)
    pallas_call x1, Pallas kernels, shards(): pl.pallas_call(functools.partial(prior_kernel, n, local_m, share), out_sh...  16.7 us
    pallas_call x1, Pallas kernels, shards(): pl.pallas_call(functools.partial(gather_kernel, n, share), out_shape=(sha...  14.7 us
    pallas_call x1, Pallas kernels, shards(): pl.pallas_call(functools.partial(reduce_kernel, n, pols), out_shape=shape...  11.5 us
    unnamed x14, local copies, waits for them, and re-layouts  9.54 us

profile of v1, /device:TPU:0, one launch (start us, length us, event | category | flops | bytes accessed | tf_op | source)
XLA Modules:
  0.0 55.3 jit_solution(9487999961186428567)
XLA Ops:
  0.0 1.3 %copy.8.limit_ref = s32[8,2]{1,0:T(8,128)} copy(s32[8,2]{0,1:T(2,128)} %param.11) | data formatting | bytes 128 | tf_op args[5]
  1.3 0.7 %broadcast_in_dim.11 = s32[8,8]{1,0:T(8,128)S(1)} reshape(s32[64]{0:T(128)} %param.10) | data formatting | bytes 512 | tf_op jit(solution)/shard_map/broadcast_in_dim | solution.py:403
  2.1 0.6 %broadcast_in_dim_reshape.7.turned_ref = s32[1,128]{1,0:T(1,128)} reshape(s32[8,2,8]{2,1,0:T(2,128)S(1)} %broadcast_in_dim.12) | data formatting | bytes 1024 | tf_op jit(solution)/shard_map/broadcast_in_dim;reshape | solution.py:421
  2.7 0.7 %copy.7.order_ref = s32[64,1]{1,0:T(8,128)S(1)} copy(s32[64,1]{0,1:T(1,128)} %bitcast.3) | data formatting | bytes 512 | tf_op jit(solution)/shard_map/broadcast_in_dim | solution.py:400
  3.4 0.7 %broadcast_in_dim_reshape.8.order_ref = s32[128,1]{1,0:T(8,128)} reshape(s32[8,2,8]{2,1,0:T(2,128)S(1)} %broadcast_in_dim.12) | data formatting | bytes 1024 | tf_op jit(solution)/shard_map/broadcast_in_dim;reshape | solution.py:421
  4.1 0.0 copy-start
  4.1 3.4 %copy-done = bf16[8,128,4096]{2,1,0:T(8,128)(2,1)S(1)} copy-done((bf16[8,128,4096]{2,1,0:T(8,128)(2,1)S(1)}, bf16[8,128,4096]{2,1,0:T(8,128)(2,1)}, u32[]{:S(2)}) %copy-start) | copy-done | bytes 8388632
  7.5 0.0 copy-start.3
  7.5 0.8 %copy-done.3 = bf16[8,4096]{1,0:T(8,128)(2,1)S(1)} copy-done((bf16[8,4096]{1,0:T(8,128)(2,1)S(1)}, bf16[8,4096]{1,0:T(8,128)(2,1)}, u32[]{:S(2)}) %copy-start.3) | copy-done | bytes 65560
  8.3 0.0 copy-start.4
  8.3 0.7 %copy-done.4 = bf16[8,128]{1,0:T(8,128)(2,1)S(1)} copy-done((bf16[8,128]{1,0:T(8,128)(2,1)S(1)}, bf16[8,128]{1,0:T(8,128)(2,1)}, u32[]{:S(2)}) %copy-start.4) | copy-done | bytes 2072
  9.0 0.0 copy-start.5
  9.0 0.7 %copy-done.5 = s32[8]{0:T(128)S(1)} copy-done((s32[8]{0:T(128)S(1)}, s32[8]{0:T(128)}, u32[]{:S(2)}) %copy-start.5) | copy-done | bytes 56
  9.7 14.7 %shard_map.64 = (bf16[2,8,16,1024]{3,2,1,0:T(8,128)(2,1)S(1)}, f32[4,8,1024]{2,1,0:T(8,128)S(1)}) custom-call(bf16[8,4096]{1,0:T(8,128)(2,1)S(1)} %copy-done.3, s32[64,1]{1,0:T(8,128)S(1)} %copy.7.order_ref, bf16[8,128]{1,0:T(8,128)(2,1)S(1)} %copy-done.4, s32[8]{0:T(128)S(1)} %copy-done.5, bf16[8,128,4096]{2,1,0:T(8,128)(2,1)S(1)} %copy-done), custom_call_target="tpu_custom_call" | custom-call | tf_op jit(solution)/shard_map/pallas_call | solution.py:384
  24.4 0.0 copy-start.2
  24.4 0.8 %copy-done.2 = bf16[2,8,16,1024]{3,2,1,0:T(8,128)(2,1)} copy-done((bf16[2,8,16,1024]{3,2,1,0:T(8,128)(2,1)}, bf16[2,8,16,1024]{3,2,1,0:T(8,128)(2,1)S(1)}, u32[]{:S(2)}) %copy-start.2) | copy-done | bytes 524312
  25.2 16.7 %shard_map.65.prior_ref = f32[4,8,8,1024]{3,2,1,0:T(8,128)} custom-call(bf16[2,128,1024]{2,1,0:T(8,128)(2,1)} %bitcast.2, s32[8,2]{1,0:T(8,128)} %copy.8.limit_ref, s32[128,1]{1,0:T(8,128)} %broadcast_in_dim_reshape.8.order_ref, s32[1,128]{1,0:T(1,128)} %broadcast_in_dim_reshape.7.turned_ref), custom_call_target="tpu_custom_call" | custom-call | tf_op jit(solution)/shard_map/pallas_call | solution.py:404
  42.0 0.0 copy-start.1
  42.0 1.2 %copy-done.1 = f32[4,8,8,1024]{3,2,1,0:T(8,128)S(1)} copy-done((f32[4,8,8,1024]{3,2,1,0:T(8,128)S(1)}, f32[4,8,8,1024]{3,2,1,0:T(8,128)}, u32[]{:S(2)}) %copy-start.1) | copy-done | bytes 1048600
  43.2 11.5 %shard_map.66 = f32[8,1024]{1,0:T(8,128)S(1)} custom-call(f32[4,8,8,1024]{3,2,1,0:T(8,128)S(1)} %copy-done.1, f32[4,8,1024]{2,1,0:T(8,128)S(1)} %get-tuple-element.8.data_ref), custom_call_target="tpu_custom_call" | custom-call | tf_op jit(solution)/shard_map/pallas_call | solution.py:426
  54.7 0.6 %copy.11 = f32[8,1024]{1,0:T(8,128)} copy(f32[8,1024]{1,0:T(8,128)S(1)} %shard_map.66) | data formatting | bytes 65536
  (1 shorter events, 0.0 us)
Async XLA Ops:
  4.1 3.4 %copy-start = (bf16[8,128,4096]{2,1,0:T(8,128)(2,1)S(1)}, bf16[8,128,4096]{2,1,0:T(8,128)(2,1)}, u32[]{:S(2)}) copy-start(bf16[8,128,4096]{2,1,0:T(8,128)(2,1)} %beam_ref.1) | copy-start | bytes 25165828
  7.5 0.8 %copy-start.3 = (bf16[8,4096]{1,0:T(8,128)(2,1)S(1)}, bf16[8,4096]{1,0:T(8,128)(2,1)}, u32[]{:S(2)}) copy-start(bf16[8,4096]{1,0:T(8,128)(2,1)} %sky_ref.1) | copy-start | bytes 196612
  8.3 0.7 %copy-start.4 = (bf16[8,128]{1,0:T(8,128)(2,1)S(1)}, bf16[8,128]{1,0:T(8,128)(2,1)}, u32[]{:S(2)}) copy-start(bf16[8,128]{1,0:T(8,128)(2,1)} %vis_ref.1) | copy-start | bytes 6148
  9.0 0.7 %copy-start.5 = (s32[8]{0:T(128)S(1)}, s32[8]{0:T(128)}, u32[]{:S(2)}) copy-start(s32[8]{0:T(128)} %count_ref.1) | copy-start | bytes 100
  24.4 0.8 %copy-start.2 = (bf16[2,8,16,1024]{3,2,1,0:T(8,128)(2,1)}, bf16[2,8,16,1024]{3,2,1,0:T(8,128)(2,1)S(1)}, u32[]{:S(2)}) copy-start(bf16[2,8,16,1024]{3,2,1,0:T(8,128)(2,1)S(1)} %get-tuple-element.7) | copy-start | bytes 1572868
  42.0 1.2 %copy-start.1 = (f32[4,8,8,1024]{3,2,1,0:T(8,128)S(1)}, f32[4,8,8,1024]{3,2,1,0:T(8,128)}, u32[]{:S(2)}) copy-start(f32[4,8,8,1024]{3,2,1,0:T(8,128)} %shard_map.65.prior_ref) | copy-start | bytes 3145732

commit v2 on v1

v2 whole, which is shorter than its diff:
```python
import functools
import math

import jax
import jax.numpy as jnp
from jax import lax
from jax.experimental import pallas as pl
from jax.experimental.pallas import tpu as pltpu
from jax.sharding import PartitionSpec as P

L = 2048
J = 8
CYCLES = 2 * L
FINE_ELL = 32
PIX_FINE = 128
PIX_TILE = 512
MESH = pl.DeviceIdType.MESH

smoothing = 0.1
prior_weight = 0.2


def short_waves(angle):
    z = angle * angle
    sine = angle * (1.0 + z * (-1.0 / 6 + z * (1.0 / 120 + z * (-1.0 / 5040 + z / 362880.0))))
    cosine = 1.0 + z * (
        -0.5 + z * (1.0 / 24 + z * (-1.0 / 720 + z * (1.0 / 40320 - z / 3628800.0)))
    )
    return cosine, sine


def turn(steps, period):
    centred = jnp.bitwise_and(steps, period - 1) - period // 2
    cosine, sine = short_waves(centred.astype(jnp.float32) * (0.5 * math.pi / period))
    cosine, sine = 1.0 - 2.0 * sine * sine, 2.0 * sine * cosine
    return 2.0 * sine * sine - 1.0, -2.0 * sine * cosine


def band_row(low, high):
    ell = lax.broadcasted_iota(jnp.int32, (1, L), 1)
    span = jnp.broadcast_to(high - low, (1, L)).astype(jnp.float32)
    fraction = (ell - low).astype(jnp.float32) / span
    inside = (ell >= low) & (ell <= high)
    cosine, sine = short_waves(0.5 * math.pi * (jnp.where(inside, fraction, 0.5) - 0.5))
    return jnp.where(inside, (1.0 - 2.0 * sine * sine) ** 2, 0.0)


def kernel(
    n, pols, sky_hbm, vis_hbm, limit_ref, order_ref, count_ref, beam_ref, out_ref,
    sky_ref, vis_ref, sky_rows, vis_rows, beam_buf, all_ref, data, data_in,
    tab, four, fort, coarse_cos, coarse_sin, kern, scaled, synth, total,
    prior_ref, mate_in, sums, peer_in,
    sky_sem, beam_sem, send1, recv1, send2, recv2, send_a, recv_a, send_b, recv_b, send_d, recv_d,
):
    ma = lax.axis_index("ma")
    pol = lax.axis_index("pol")
    side = lax.rem(pol, 2)
    mate = pol + 1 - 2 * side
    pairs = pols // 2
    pair = pol // 2
    everyone = n * pairs
    place = ma * pairs + pair
    local_m, modes, width = beam_buf.shape
    share = out_ref.shape[1]
    rows = four.shape[0]
    cycles = tab.shape[1]
    scales = synth.shape[0] // rows

    def beam_copy(i):
        return pltpu.make_async_copy(beam_ref.at[i], beam_buf.at[i], beam_sem.at[i])

    def sky_copy():
        return pltpu.make_async_copy(sky_hbm, sky_ref, sky_sem.at[0])

    def vis_copy():
        return pltpu.make_async_copy(vis_hbm, vis_ref, sky_sem.at[1])

    def sky_peer(d):
        return pltpu.make_async_remote_copy(
            src_ref=all_ref.at[side, ma], dst_ref=all_ref.at[side, ma],
            send_sem=send1.at[d], recv_sem=recv1.at[d],
            device_id=(lax.rem(ma + d, n), pol), device_id_type=MESH,
        )

    def sky_mate(d):
        source = lax.rem(ma + n - d, n)
        return pltpu.make_async_remote_copy(
            src_ref=all_ref.at[side, source], dst_ref=all_ref.at[side, source],
            send_sem=send2.at[d], recv_sem=recv2.at[d],
            device_id=(ma, mate), device_id_type=MESH,
        )

    def data_copy(d):
        other = lax.rem(pol + d, pols)
        return pltpu.make_async_remote_copy(
            src_ref=data.at[other], dst_ref=data_in.at[d - 1],
            send_sem=send_d.at[d - 1], recv_sem=recv_d.at[d - 1],
            device_id=(ma, other), device_id_type=MESH,
        )

    def mate_copy(h):
        return pltpu.make_async_remote_copy(
            src_ref=prior_ref.at[2 * h + 1 - side], dst_ref=mate_in.at[h],
            send_sem=send_a.at[h], recv_sem=recv_a.at[h],
            device_id=(ma, mate), device_id_type=MESH,
        )

    def peer_copy(d):
        target = lax.rem(place + d, everyone)
        target_ma = target // pairs
        target_pair = lax.rem(target, pairs)
        return pltpu.make_async_remote_copy(
            src_ref=sums.at[target_pair, target_ma], dst_ref=peer_in.at[d - 1],
            send_sem=send_b.at[d - 1], recv_sem=recv_b.at[d - 1],
            device_id=(target_ma, 2 * target_pair + side), device_id_type=MESH,
        )

    sky_copy().start()
    vis_copy().start()
    for i in range(local_m):
        beam_copy(i).start()

    barrier = pltpu.get_barrier_semaphore()

    @pl.loop(1, everyone)
    def _(d):
        target = lax.rem(place + d, everyone)
        pl.semaphore_signal(
            barrier, inc=1,
            device_id=(target // pairs, 2 * lax.rem(target, pairs) + side), device_id_type=MESH,
        )

    for d in range(1, pols, 2):
        pl.semaphore_signal(
            barrier, inc=1, device_id=(ma, lax.rem(pol + d, pols)), device_id_type=MESH
        )
    orders = jnp.zeros((local_m, 1), jnp.int32)
    for i in range(local_m):
        orders = jnp.where(
            lax.broadcasted_iota(jnp.int32, (local_m, 1), 0) == i, order_ref[ma * local_m + i], orders
        )
    sky_copy().wait()
    vis_copy().wait()
    alive = lax.rem(lax.broadcasted_iota(jnp.int32, (1, width), 1), L) >= orders
    masked = jnp.where(alive, sky_ref[...].astype(jnp.float32), 0.0)
    half = L // 2
    for h in range(2):
        all_ref[h, ma] = jnp.concatenate(
            [masked[:, h * half : (h + 1) * half], masked[:, L + h * half : L + (h + 1) * half]],
            axis=0,
        ).astype(jnp.bfloat16)
    vis = vis_ref[...].astype(jnp.float32)
    for i in range(local_m):
        sky_rows[i] = masked[i : i + 1]
        vis_rows[i] = vis[i : i + 1]

    pl.semaphore_wait(barrier, everyone - 1 + pairs)

    @pl.loop(1, n)
    def _(d):
        sky_peer(d).start()

    amplitude = math.sqrt(2.0 / L)
    norm = 1.0 / math.sqrt(rows // 2)

    def index(count, axis):
        return lax.broadcasted_iota(jnp.int32, (count, 1) if axis == 0 else (1, count), axis)

    table_rows = lax.broadcasted_iota(jnp.int32, (limit_ref.shape[0], 1), 0)
    for j in range(scales):
        low, high = [
            jnp.sum(
                jnp.where(table_rows == pol * scales + j, limit_ref[:, e : e + 1], 0),
                axis=0, keepdims=True,
            )
            for e in range(2)
        ]
        kern[j] = band_row(low, high)
    down_row, across_row = index(rows, 0), index(rows, 1)
    down_row = (down_row // (2 * local_m)) * local_m + lax.rem(down_row, local_m)
    across_row = (across_row // (2 * local_m)) * local_m + lax.rem(across_row, local_m)

    def place_order(i, found):
        order = order_ref[i]
        return (
            jnp.where(down_row == i, order, found[0]),
            jnp.where(across_row == i, order, found[1]),
        )

    down, across = lax.fori_loop(
        0, n * local_m, place_order, (jnp.zeros_like(down_row), jnp.zeros_like(across_row))
    )
    quarter = jnp.bitwise_and(down, 3)
    cp = jnp.where(quarter == 0, 1.0, jnp.where(quarter == 2, -1.0, 0.0))
    sp = jnp.where(quarter == 1, 1.0, jnp.where(quarter == 3, -1.0, 0.0))
    odd = 2 * (ma * cycles + index(cycles, 1)) + 1
    _, weight = turn(odd, 4 * CYCLES)

    period = 8 * CYCLES
    blocks = L // FINE_ELL
    coarse = 2 * FINE_ELL * index(blocks, 0) * odd - CYCLES
    for part in range(2):
        cosine, sine = turn(coarse - part * (period // 4), period)
        for b in range(blocks):
            coarse_cos[part * blocks + b] = amplitude * cosine[b : b + 1]
            coarse_sin[part * blocks + b] = amplitude * sine[b : b + 1]
    fine_cos, fine_sin = turn((2 * index(FINE_ELL, 0) + 1) * odd, period)

    @pl.loop(0, 2 * blocks)
    def _(b):
        at = pl.ds(pl.multiple_of(b * FINE_ELL, FINE_ELL), FINE_ELL)
        tab[at, :] = (fine_cos * coarse_cos[b] - fine_sin * coarse_sin[b]).astype(jnp.bfloat16)

    steps = CYCLES // PIX_FINE
    quarter_turn = CYCLES // 4
    down_part = lax.rem(index(rows, 0) // local_m, 2) * quarter_turn
    across_part = lax.rem(index(rows, 1) // local_m, 2) * quarter_turn
    down_fine = turn(down * index(PIX_FINE, 1), CYCLES)
    down_coarse = turn(down * (PIX_FINE * index(steps, 1)) + down_part, CYCLES)
    across_fine = turn(across * index(PIX_FINE, 0), CYCLES)
    across_coarse = turn(across * (PIX_FINE * index(steps, 0)) + across_part, CYCLES)
    down_fine = [norm * part for part in down_fine]
    across_fine = [norm * part for part in across_fine]
    for b in range(steps):
        at = slice(b * PIX_FINE, (b + 1) * PIX_FINE)
        four[:, at] = (
            down_fine[0] * down_coarse[0][:, b : b + 1]
            - down_fine[1] * down_coarse[1][:, b : b + 1]
        ).astype(jnp.bfloat16)
        fort[at, :] = (
            across_fine[0] * across_coarse[0][b : b + 1, :]
            - across_fine[1] * across_coarse[1][b : b + 1, :]
        ).astype(jnp.bfloat16)

    mode_index = pol * modes + lax.broadcasted_iota(jnp.int32, (modes, 1), 0)
    diagonal = lax.broadcasted_iota(jnp.int32, (modes, modes), 0) == lax.broadcasted_iota(
        jnp.int32, (modes, modes), 1
    )

    def one_order(i):
        beam_copy(i).wait()
        mine = lax.broadcasted_iota(jnp.int32, (local_m, 1), 0) == i
        total = jnp.where(diagonal, -vis_rows[i], 0.0)
        for t in range(0, width, 128):
            row = sky_rows[i, :, t : t + 128]
            total = total + beam_buf[i, :, t : t + 128].astype(jnp.float32) * row
        image = jnp.sum(total, axis=1, keepdims=True)
        misfit = jnp.where(mode_index < count_ref[i], image, 0.0)
        spread = jnp.broadcast_to(
            misfit.astype(jnp.bfloat16).astype(jnp.float32), (modes, 128)
        )
        for t in range(0, width, 128):
            column = jnp.sum(
                beam_buf[i, :, t : t + 128].astype(jnp.float32) * spread, axis=0, keepdims=True
            )
            b, o = t // share, t % share
            data[b, :, o : o + 128] += jnp.where(mine, column, 0.0)

    data[...] = jnp.zeros_like(data)

    @pl.loop(1, n)
    def _(d):
        sky_peer(d).wait_recv()
        sky_mate(d).start()

    @pl.loop(0, local_m)
    def _(i):
        one_order(i)

    for b in range(pols):
        ell = lax.rem(b * share + lax.broadcasted_iota(jnp.int32, (1, share), 1), L)
        data[b] = jnp.where(ell >= orders, data[b], 0.0)
    for d in range(1, pols):
        data_copy(d).start()

    @pl.loop(1, n)
    def _(d):
        sky_mate(d).wait_recv()

    for j in range(scales):
        for h in range(2):
            for d in range(n):
                scaled[2 * local_m * d : 2 * local_m * (d + 1), h * half : (h + 1) * half] = (
                    kern[j, :, h * half : (h + 1) * half] * all_ref[h, d].astype(jnp.float32)
                ).astype(jnp.bfloat16)
        with_cos = jnp.dot(scaled[...], tab[0:L, :], preferred_element_type=jnp.float32)
        with_sin = jnp.dot(scaled[...], tab[L : 2 * L, :], preferred_element_type=jnp.float32)
        synth[j * rows : (j + 1) * rows, :] = (cp * with_cos - sp * with_sin).astype(jnp.bfloat16)

    total[...] = jnp.zeros_like(total)

    @pl.loop(0, CYCLES // PIX_TILE)
    def _(t):
        at = pl.ds(pl.multiple_of(t * PIX_TILE, PIX_TILE), PIX_TILE)
        left = fort[at, :]
        right = four[:, at]
        for j in range(scales):
            mine = slice(j * rows, (j + 1) * rows)
            pixels = jnp.dot(left, synth[mine, :], preferred_element_type=jnp.float32)
            slopes = (
                weight * pixels * lax.rsqrt(pixels * pixels + smoothing * smoothing)
            ).astype(jnp.bfloat16)
            total[mine, :] += jnp.dot(right, slopes, preferred_element_type=jnp.float32)

    contract_last = (((1,), (1,)), ((), ()))

    def back(block):
        t = pl.multiple_of(block * share, share)
        ell = t + lax.broadcasted_iota(jnp.int32, (1, share), 1)
        prior = jnp.zeros((rows, share), jnp.float32)
        for j in range(scales):
            cycle_b = total[j * rows : (j + 1) * rows, :].astype(jnp.bfloat16)
            back_cos = lax.dot_general(
                cycle_b, tab[pl.ds(t, share), :], contract_last,
                preferred_element_type=jnp.float32,
            )
            back_sin = lax.dot_general(
                cycle_b, tab[pl.ds(L + t, share), :], contract_last,
                preferred_element_type=jnp.float32,
            )
            prior = prior + kern[j, :, pl.ds(t, share)] * (cp * back_cos - sp * back_sin)
        prior = jnp.where(ell >= down, prior_weight * prior, 0.0)
        for d in range(n):
            for c in range(2):
                first = (2 * d + c) * local_m
                prior_ref[c * pairs + block, d] = prior[first : first + local_m, :]

    for b in range(0, pairs, 2):
        back(b + 1 - side)
    for h in range(pairs):
        mate_copy(h).start()
    for b in range(0, pairs, 2):
        back(b + side)
    for h in range(pairs):
        mate_copy(h).wait_recv()
        both = prior_ref[2 * h + side] + mate_in[h]
        sums[h] = jnp.concatenate(
            [both[:, :, : share // 2], both[:, :, share // 2 :]], axis=1
        ).astype(jnp.bfloat16)

    @pl.loop(1, everyone)
    def _(d):
        peer_copy(d).start()

    result = data[pol] + (prior_ref[pol, ma] + mate_in[pair, ma])
    for d in range(1, pols):
        data_copy(d).wait_recv()
        result = result + data_in[d - 1]

    def add(d, running):
        peer_copy(d).wait_recv()
        return running + peer_in[d - 1].astype(jnp.float32)

    prior = lax.fori_loop(1, everyone, add, jnp.zeros(peer_in.shape[1:], jnp.float32))
    out_ref[:, : share // 2] = result[:, : share // 2] + prior[:local_m]
    out_ref[:, share // 2 :] = result[:, share // 2 :] + prior[local_m:]

    for h in range(pairs):
        mate_copy(h).wait_send()
    for d in range(1, pols):
        data_copy(d).wait_send()

    @pl.loop(1, everyone)
    def _(d):
        peer_copy(d).wait_send()

    @pl.loop(1, n)
    def _(d):
        sky_peer(d).wait_send()
        sky_mate(d).wait_send()


def shards(sky_coeffs, visibilities, beam_blocks, mode_counts, order_table, band_limits):
    local_m, width = sky_coeffs.shape
    modes = beam_blocks.shape[1]
    n = lax.axis_size("ma")
    pols = lax.axis_size("pol")
    cycles = CYCLES // n
    scales = J // pols
    share = width // pols
    pairs = pols // 2
    everyone = n * pairs
    rows = 2 * n * local_m
    piece = (2 * local_m, share // 2)
    vmem = pl.BlockSpec(memory_space=pltpu.VMEM)
    smem = pl.BlockSpec(memory_space=pltpu.SMEM)
    hbm = pl.BlockSpec(memory_space=pl.ANY)
    f32, bf16 = jnp.float32, jnp.bfloat16
    sem = pltpu.SemaphoreType.DMA
    return pl.pallas_call(
        functools.partial(kernel, n, pols),
        out_shape=jax.ShapeDtypeStruct((local_m, share), f32),
        in_specs=[hbm, hbm, vmem, smem, smem, hbm],
        out_specs=vmem,
        scratch_shapes=[
            pltpu.VMEM((local_m, width), bf16),
            pltpu.VMEM((local_m, modes), bf16),
            pltpu.VMEM((local_m, 1, width), f32),
            pltpu.VMEM((local_m, 1, modes), f32),
            pltpu.VMEM((local_m, modes, width), bf16),
            pltpu.VMEM((2, n, 2 * local_m, L // 2), bf16),
            pltpu.VMEM((pols, local_m, share), f32),
            pltpu.VMEM((pols - 1, local_m, share), f32),
            pltpu.VMEM((2 * L, cycles), bf16),
            pltpu.VMEM((rows, CYCLES), bf16),
            pltpu.VMEM((CYCLES, rows), bf16),
            pltpu.VMEM((2 * L // FINE_ELL, 1, cycles), f32),
            pltpu.VMEM((2 * L // FINE_ELL, 1, cycles), f32),
            pltpu.VMEM((scales, 1, L), f32),
            pltpu.VMEM((rows, L), bf16),
            pltpu.VMEM((scales * rows, cycles), bf16),
            pltpu.VMEM((scales * rows, cycles), f32),
            pltpu.VMEM((pols, n, local_m, share), f32),
            pltpu.VMEM((pairs, n, local_m, share), f32),
            pltpu.VMEM((pairs, n) + piece, bf16),
            pltpu.VMEM((everyone - 1,) + piece, bf16),
            sem((2,)), sem((local_m,)),
            sem((n,)), sem((n,)), sem((n,)), sem((n,)),
            sem((pairs,)), sem((pairs,)),
            sem((everyone - 1,)), sem((everyone - 1,)),
            sem((pols - 1,)), sem((pols - 1,)),
        ],
        compiler_params=pltpu.CompilerParams(
            collective_id=0, has_side_effects=True, vmem_limit_bytes=60 * 2**20
        ),
    )(sky_coeffs, visibilities, band_limits, order_table, mode_counts, beam_blocks)


def solution(mesh):
    placed = (P("ma", None), P("ma", "pol"), P("ma", "pol", None), P("ma"), P(), P())
    return jax.shard_map(
        shards, mesh=mesh, in_specs=placed, out_specs=P("ma", "pol"), check_vma=False
    )
```

time: 56.4 us -> 40.5 us (0.72); the launches traced: 55.3 us -> 40.3 us
  local copies, waits for them, and re-layouts: 12.3 us -> 2.72 us
  Pallas kernels: 42.9 us -> 37.6 us
    unnamed x14 -> x2, local copies, waits for them, and re-layouts: 9.54 us -> 2.72 us
    pallas_call x3 -> x1, Pallas kernels: 42.9 us -> 37.6 us  [shards(): pl.pallas_call(functools.partial(kernel, n, pols), out_shape=jax.ShapeDty...]
    broadcast_in_dim x3 -> x0, local copies, waits for them, and re-layouts: 1.48 us -> none  [the longest x1 0.74 us: shards(): order_table[:, None]]
    another operation x2 -> x0, local copies, waits for them, and re-layouts: 1.29 us -> none  [the longest x1 0.71 us: shards(): row_orders[:, None]]
where the time goes in v2:
time: 40.5 us; the launch traced here: 40.3 us
  Pallas kernels  37.6 us (93%)
  local copies, waits for them, and re-layouts  2.72 us (7%)
    pallas_call x1, Pallas kernels, shards(): pl.pallas_call(functools.partial(kernel, n, pols), out_shape=jax.ShapeDty...  37.6 us
    unnamed x2, local copies, waits for them, and re-layouts  2.72 us

profile of v2, /device:TPU:0, one launch (start us, length us, event | category | flops | bytes accessed | tf_op | source)
XLA Modules:
  0.0 40.3 jit_solution(15511791848859669743)
XLA Ops:
  0.0 1.3 %copy.7.limit_ref = s32[8,2]{1,0:T(8,128)} copy(s32[8,2]{0,1:T(2,128)} %param.11) | data formatting | bytes 128 | tf_op args[5]
  1.3 37.6 %shard_map.64 = f32[8,1024]{1,0:T(8,128)} custom-call(bf16[8,4096]{1,0:T(8,128)(2,1)} %sky_hbm.1, bf16[8,128]{1,0:T(8,128)(2,1)} %vis_hbm.1, s32[8,2]{1,0:T(8,128)} %copy.7.limit_ref, s32[64]{0:T(128)} %order_ref.1, s32[8]{0:T(128)} %count_ref.1, bf16[8,128,4096]{2,1,0:T(8,128)(2,1)} %beam_ref.1), custom_call_target="tpu_custom_call" | custom-call | tf_op jit(solution)/shard_map/pallas_call | solution.py:390
  38.9 1.4 %copy.9 = f32[8,1024]{1,0:T(8,128)} copy(f32[8,1024]{1,0:T(8,128)} %shard_map.64) | data formatting | bytes 65536

commit v3 on v2

--- a/solution.py
+++ b/solution.py
@@ -166,13 +166,16 @@
     def index(count, axis):
         return lax.broadcasted_iota(jnp.int32, (count, 1) if axis == 0 else (1, count), axis)
 
-    table_rows = lax.broadcasted_iota(jnp.int32, (limit_ref.shape[0], 1), 0)
+    table_columns = lax.broadcasted_iota(jnp.int32, (1, limit_ref.shape[1]), 1)
     for j in range(scales):
         low, high = [
             jnp.sum(
-                jnp.where(table_rows == pol * scales + j, limit_ref[:, e : e + 1], 0),
-                axis=0, keepdims=True,
-            )
+                jnp.where(
+                    table_columns == pol * scales + j,
+                    limit_ref[e : e + 1, :].astype(jnp.float32), 0.0,
+                ),
+                axis=1, keepdims=True,
+            ).astype(jnp.int32)
             for e in range(2)
         ]
         kern[j] = band_row(low, high)
@@ -257,13 +260,18 @@
             data[b, :, o : o + 128] += jnp.where(mine, column, 0.0)
 
     data[...] = jnp.zeros_like(data)
+    early = local_m // 2
+
+    @pl.loop(0, early)
+    def _(i):
+        one_order(i)
 
     @pl.loop(1, n)
     def _(d):
         sky_peer(d).wait_recv()
         sky_mate(d).start()
 
-    @pl.loop(0, local_m)
+    @pl.loop(early, local_m)
     def _(i):
         one_order(i)
 
@@ -423,7 +431,7 @@
         compiler_params=pltpu.CompilerParams(
             collective_id=0, has_side_effects=True, vmem_limit_bytes=60 * 2**20
         ),
-    )(sky_coeffs, visibilities, band_limits, order_table, mode_counts, beam_blocks)
+    )(sky_coeffs, visibilities, band_limits.T, order_table, mode_counts, beam_blocks)
 
 
 def solution(mesh):

time: 40.5 us -> 37.6 us (0.928)
  Pallas kernels: 37.6 us -> 36.1 us
  local copies, waits for them, and re-layouts: 2.72 us -> 1.38 us
    pallas_call x1, Pallas kernels: 37.6 us -> 36.1 us  [shards(): pl.pallas_call(functools.partial(kernel, n, pols), out_shape=jax.ShapeDty...]
    unnamed x2 -> x1, local copies, waits for them, and re-layouts: 2.72 us -> 1.38 us
where the time goes in v3:
time: 37.6 us; the launch traced here: 37.5 us
  Pallas kernels  36.1 us (96%)
  local copies, waits for them, and re-layouts  1.38 us (4%)
    pallas_call x1, Pallas kernels, shards(): pl.pallas_call(functools.partial(kernel, n, pols), out_shape=jax.ShapeDty...  36.1 us
    unnamed x1, local copies, waits for them, and re-layouts  1.38 us

profile of v3, /device:TPU:0, one launch (start us, length us, event | category | flops | bytes accessed | tf_op | source)
XLA Modules:
  0.0 37.5 jit_solution(1140537889161111398)
XLA Ops:
  0.0 36.1 %shard_map.64 = f32[8,1024]{1,0:T(8,128)} custom-call(bf16[8,4096]{1,0:T(8,128)(2,1)} %sky_hbm.1, bf16[8,128]{1,0:T(8,128)(2,1)} %vis_hbm.1, s32[2,8]{1,0:T(2,128)} %bitcast.1, s32[64]{0:T(128)} %order_ref.1, s32[8]{0:T(128)} %count_ref.1, bf16[8,128,4096]{2,1,0:T(8,128)(2,1)} %beam_ref.1), custom_call_target="tpu_custom_call" | custom-call | tf_op jit(solution)/shard_map/pallas_call | solution.py:398
  36.1 1.4 %copy.8 = f32[8,1024]{1,0:T(8,128)} copy(f32[8,1024]{1,0:T(8,128)} %shard_map.64) | data formatting | bytes 65536
